TPU v7x, 32 devices: a whole 2x2x4 slice. The times are simulated.
32 devices in a mesh: user: 16 (over z, y, x), item: 2 (over core).
Axes of the slice: x: 2, y: 2, z: 4, core: 2. Of those that a mesh axis runs over, the one named last changes fastest.
Arguments:
- user_factors: bfloat16 [16384, 256], P('user'), may hold values from -0.3984375 to 0.3984375
- item_panels: float32 [32768, 256], P(('user', 'item')), may hold values from -6 to 6
- ratings: bfloat16 [3, 384, 256, 128], P(None, 'user', 'item'), may hold values from -6 to 6
- tile_ids: int32 [3, 384, 2], P(None, 'user', 'item'), may hold values from 0 to 63, as said below
- tile_count: int32 [3, 16, 2], P(None, 'user', 'item'), may hold values from 6 to 24, as said below
Outputs:
- panels_out: float32 [32768, 256], P(('user', 'item'))
- user_grad: float32 [16384, 256], P(('user', 'item'))
Inputs may be any that keep to these rules, and one draw needn't show every extreme that they name: `tile_ids`: the first 24 entries of each user block's list for a group and step are distinct tiles of the block. `tile_count`: in every step some user block and group has all 24 slots live.
All inputs are finite; a program needn't handle non-finite values.
Results may differ from a plain program's by a relative error of at most 0.0013.
Values sent between devices are 32-bit elements; how exact they have to be, the bound alone decides.
A program may use at most 64 MiB of HBM per device.

v0:
```python
import functools

import jax
import jax.numpy as jnp
from jax import lax
from jax.experimental import pallas as pl
from jax.experimental.pallas import tpu as pltpu
from jax.sharding import PartitionSpec as P

TILE = 128
CHUNK = 128
BLOCK = 256
FLIGHT = 2
PIECES = 4
MESH = pl.DeviceIdType.MESH

learn_rate = 0.05
weight_decay = 0.02
user_scale = 1.0 / 64.0


def kernel(
    steps, cycle, groups,
    ids_ref, count_ref, users_hbm, panel_hbm, ratings_hbm, panel_out, grad_out,
    slot_rows, slot_ref, users, total, residual, grad_in, held, ratings,
    load_sem, rate_sem, slot_sem, send_sem, recv_sem, out_sem, grad_send, grad_recv,
):
    rows, rank = users.shape
    items = held[0].shape[0]
    slots = ratings[0].shape[0]
    row_tiles, col_tiles = rows // TILE, items // TILE
    chunks = items // CHUNK
    wide = CHUNK // TILE
    share = rows // groups

    u = lax.axis_index("user")
    g = lax.axis_index("item")
    right, left = lax.rem(u + 1, cycle), lax.rem(u + cycle - 1, cycle)

    barrier = pltpu.get_barrier_semaphore()
    pl.semaphore_signal(barrier, inc=1, device_id={"user": left}, device_id_type=MESH)
    for d in range(1, groups):
        pl.semaphore_signal(
            barrier, inc=1, device_id={"item": lax.rem(g + d, groups)}, device_id_type=MESH
        )

    def part(c):
        return pl.ds(pl.multiple_of(c * CHUNK, CHUNK), CHUNK)

    load_users = pltpu.make_async_copy(users_hbm, users, load_sem.at[chunks])
    load_panel = [
        pltpu.make_async_copy(panel_hbm.at[part(c)], held[0].at[part(c)], load_sem.at[c])
        for c in range(chunks)
    ]
    load_rates = [
        pltpu.make_async_copy(ratings_hbm.at[s], ratings[s], rate_sem.at[s]) for s in range(steps)
    ]
    load_panel[0].start()
    load_users.start()
    load_rates[0].start()
    for c in range(1, chunks):
        load_panel[c].start()
    for s in range(1, steps):
        load_rates[s].start()

    def send(s, c):
        return pltpu.make_async_remote_copy(
            src_ref=held[s].at[part(c)],
            dst_ref=held[s + 1].at[part(c)],
            send_sem=send_sem.at[s, c],
            recv_sem=recv_sem.at[s, c],
            device_id={"user": right},
            device_id_type=MESH,
        )

    def write(c):
        return pltpu.make_async_copy(held[-1].at[part(c)], panel_out.at[part(c)], out_sem.at[c])

    tile = lax.broadcasted_iota(jnp.int32, (1, slot_rows.shape[1]), 1)
    for s in range(steps):
        slot_of = jnp.full(tile.shape, slots, jnp.int32)
        for k in range(slots):
            listed = jnp.where(k < count_ref[s], ids_ref[s, 0, k], -1)
            slot_of = jnp.where(tile == listed, k, slot_of)
        slot_rows[s : s + 1, :] = slot_of
    map_slots = pltpu.make_async_copy(slot_rows, slot_ref, slot_sem)
    map_slots.start()

    def residuals(s, c, rounded):
        for top in range(0, rows, BLOCK):
            predicted = lax.dot_general(
                users[top : top + BLOCK, :], rounded, (((1,), (1,)), ((), ())),
                preferred_element_type=jnp.float32,
            )
            for i in range(BLOCK // TILE):
                for j in range(wide):
                    slot = slot_ref[s, (top // TILE + i) * col_tiles + c * wide + j]
                    live = (slot < slots).astype(jnp.float32)
                    rated = ratings[s][jnp.minimum(slot, slots - 1)].astype(jnp.float32)
                    guess = predicted[i * TILE : (i + 1) * TILE, j * TILE : (j + 1) * TILE]
                    residual[
                        top + i * TILE : top + (i + 1) * TILE, j * TILE : (j + 1) * TILE
                    ] = ((guess - rated) * live).astype(jnp.bfloat16)

    def update(s, c, panel):
        item_grad = lax.dot_general(
            residual[...], users[...], (((0,), (0,)), ((), ())),
            preferred_element_type=jnp.float32,
        )
        held[s][part(c), :] = panel - learn_rate * (item_grad + weight_decay * panel)

    def add_users(rounded, start, size):
        step = min(size, BLOCK)
        for offset in range(0, size, step):
            here = pl.ds(pl.multiple_of(start + offset, step), step)
            total[here, :] += jnp.dot(
                residual[here, :], rounded, preferred_element_type=jnp.float32
            )

    total[...] = jnp.zeros_like(total)
    map_slots.wait()
    load_users.wait()
    for s in range(steps):
        load_rates[s].wait()

        def work(c, carry, s=s):
            if s == 0:
                pltpu.make_async_copy(
                    panel_hbm.at[part(c)], held[0].at[part(c)], load_sem.at[c]
                ).wait()
            else:
                send(s - 1, c).wait_recv()
            panel = held[s][part(c), :]
            rounded = panel.astype(jnp.bfloat16)
            residuals(s, c, rounded)
            update(s, c, panel)
            if s < steps - 1:
                if s == 0:
                    @pl.when(c == 0)
                    def _():
                        pl.semaphore_wait(barrier, groups)

                    @pl.when(c >= FLIGHT)
                    def _():
                        send(0, c - FLIGHT).wait_send()
                else:
                    @pl.when(c >= FLIGHT)
                    def _():
                        send(s, c - FLIGHT).wait_send()

                    @pl.when(c < FLIGHT)
                    def _():
                        send(s - 1, chunks + c - FLIGHT).wait_send()
                send(s, c).start()
            else:
                write(c).start()
            add_users(rounded, 0, rows)
            return carry

        lax.fori_loop(0, chunks if s < steps - 1 else chunks - 1, work, 0)

    def exchange(d):
        peer = lax.rem(g + d, groups)
        return pltpu.make_async_remote_copy(
            src_ref=total.at[pl.ds(pl.multiple_of(peer * share, share), share)],
            dst_ref=grad_in.at[d - 1],
            send_sem=grad_send.at[d - 1],
            recv_sem=grad_recv.at[d - 1],
            device_id={"item": peer},
            device_id_type=MESH,
        )

    final, last = steps - 1, chunks - 1
    send(final - 1, last).wait_recv()
    panel = held[final][part(last), :]
    rounded = panel.astype(jnp.bfloat16)
    residuals(final, last, rounded)
    for d in range(1, groups):
        add_users(rounded, lax.rem(g + d, groups) * share, share)
        exchange(d).start()
    update(final, last, panel)
    write(last).start()
    add_users(rounded, g * share, share)
    mine = pl.ds(pl.multiple_of(g * share, share), share)
    for d in range(1, groups):
        exchange(d).wait_recv()
        total[mine, :] += grad_in[d - 1]
    total[mine, :] = user_scale * total[mine, :]
    finish = pltpu.make_async_copy(total.at[mine], grad_out, load_sem.at[chunks])
    finish.start()
    for d in range(1, groups):
        exchange(d).wait_send()
    for c in range(chunks - FLIGHT, chunks):
        send(final - 1, c).wait_send()
    for c in range(chunks):
        write(c).wait()
    finish.wait()


def place(held, gradient, panel_out, grad_out, panel_sem, grad_sem):
    copies = []
    for source, target, sem in ((held, panel_out, panel_sem), (gradient, grad_out, grad_sem)):
        size = source.shape[0] // PIECES
        for piece in range(PIECES):
            here = pl.ds(piece * size, size)
            copies.append(
                pltpu.make_async_copy(source.at[here], target.at[here], sem.at[piece])
            )
    for copy in copies:
        copy.start()
    for copy in copies:
        copy.wait()


def shards(user_factors, item_panels, ratings, tile_ids, tile_count):
    cycle, groups = lax.axis_size("user"), lax.axis_size("item")
    rows, rank = user_factors.shape
    items = item_panels.shape[0]
    steps, slots = ratings.shape[:2]
    chunks = items // CHUNK
    tiles = (rows // TILE) * (items // TILE)
    share = rows // groups

    ids = tile_ids.reshape(steps, 1, slots)
    count = tile_count.reshape(steps)

    scalars = pl.BlockSpec(memory_space=pltpu.SMEM)
    distant = pl.BlockSpec(memory_space=pltpu.HBM)
    anywhere = pl.BlockSpec(memory_space=pl.ANY)
    held, gradient = pl.pallas_call(
        functools.partial(kernel, steps, cycle, groups),
        out_shape=(
            pltpu.VMEM((items, rank), jnp.float32),
            pltpu.VMEM((share, rank), jnp.float32),
        ),
        in_specs=[scalars] * 2 + [distant] * 3,
        out_specs=(anywhere, anywhere),
        scratch_shapes=[
            pltpu.VMEM((steps, tiles), jnp.int32),
            pltpu.SMEM((steps, tiles), jnp.int32),
            pltpu.VMEM((rows, rank), jnp.bfloat16),
            pltpu.VMEM((rows, rank), jnp.float32),
            pltpu.VMEM((rows, CHUNK), jnp.bfloat16),
            pltpu.VMEM((max(groups - 1, 1), share, rank), jnp.float32),
            [pltpu.VMEM((items, rank), jnp.float32) for _ in range(steps)],
            [pltpu.VMEM((slots, TILE, TILE), jnp.bfloat16) for _ in range(steps)],
            pltpu.SemaphoreType.DMA((chunks + 1,)),
            pltpu.SemaphoreType.DMA((steps,)),
            pltpu.SemaphoreType.DMA,
            pltpu.SemaphoreType.DMA((steps - 1, chunks)),
            pltpu.SemaphoreType.DMA((steps - 1, chunks)),
            pltpu.SemaphoreType.DMA((chunks,)),
            pltpu.SemaphoreType.DMA((max(groups - 1, 1),)),
            pltpu.SemaphoreType.DMA((max(groups - 1, 1),)),
        ],
        compiler_params=pltpu.CompilerParams(
            collective_id=0, has_side_effects=True, vmem_limit_bytes=56 * 2**20
        ),
        name="sub_epoch",
    )(
        ids, count,
        *(pltpu.with_memory_space_constraint(x, pltpu.HBM) for x in (user_factors, item_panels, ratings)),
    )
    return pl.pallas_call(
        place,
        out_shape=(
            jax.ShapeDtypeStruct(held.shape, held.dtype),
            jax.ShapeDtypeStruct(gradient.shape, gradient.dtype),
        ),
        in_specs=[anywhere] * 2,
        out_specs=(anywhere, anywhere),
        scratch_shapes=[pltpu.SemaphoreType.DMA((PIECES,)), pltpu.SemaphoreType.DMA((PIECES,))],
        name="place",
    )(held, gradient)


def solution(mesh):
    in_specs = (
        P("user", None),
        P(("user", "item"), None),
        P(None, "user", "item", None),
        P(None, "user", "item"),
        P(None, "user", "item"),
    )
    out_specs = (P(("user", "item"), None), P(("user", "item"), None))
    return jax.shard_map(shards, mesh=mesh, in_specs=in_specs, out_specs=out_specs, check_vma=False)
```

profile of v0, /device:TPU:0, one launch (start us, length us, event | category | flops | bytes accessed | tf_op | source)
XLA Modules:
  0.0 109.1 jit_solution(12577195230279524281)
XLA Ops:
  0.6 57.9 %sub_epoch.1 = (f32[1024,256]{1,0:T(8,128)S(1)}, f32[512,256]{1,0:T(8,128)S(1)}) custom-call(s32[3,1,24]{2,1,0:T(1,128)} %bitcast.2, s32[3]{0:T(128)} %bitcast.3, bf16[1024,256]{1,0:T(8,128)(2,1)} %users_hbm.1, f32[1024,256]{1,0:T(8,128)} %panel_hbm.1, bf16[3,24,128,128]{3,2,1,0:T(8,128)(2,1)} %ratings_hbm.1), custom_call_target="tpu_custom_call" | custom-call | tf_op jit(solution)/shard_map/sub_epoch/pallas_call | solution.py:230
  58.5 0.0 copy-start
  58.5 1.0 copy-done
  59.5 0.0 copy-start.1
  59.5 0.8 copy-done.1
  60.3 48.8 %place.1 = (f32[1024,256]{1,0:T(8,128)}, f32[512,256]{1,0:T(8,128)}) custom-call(f32[1024,256]{1,0:T(8,128)} %copy-done, f32[512,256]{1,0:T(8,128)} %copy-done.1), custom_call_target="tpu_custom_call" | custom-call | tf_op jit(solution)/shard_map/place/pallas_call | solution.py:264
Async XLA Ops:
  58.5 1.0 copy-start
  59.5 0.8 copy-start.1
where the time goes:
time: 109 us
  Pallas kernels  107 us (98%)
  local copies, waits for them, and re-layouts  1.76 us (2%)
    pallas_call x1, Pallas kernels, shards(): pl.pallas_call(functools.partial(kernel, steps, cycle, groups), out_shape...  57.9 us
    pallas_call x1, Pallas kernels, shards(): pl.pallas_call(place, out_shape=(jax.ShapeDtypeStruct(held.shape, held.dt...  48.8 us

commit v1 on v0

--- a/solution.py
+++ b/solution.py
@@ -10,7 +10,7 @@
 TILE = 128
 CHUNK = 128
 BLOCK = 256
-FLIGHT = 2
+FLIGHT = 4
 PIECES = 4
 MESH = pl.DeviceIdType.MESH
 
@@ -23,7 +23,7 @@
     steps, cycle, groups,
     ids_ref, count_ref, users_hbm, panel_hbm, ratings_hbm, panel_out, grad_out,
     slot_rows, slot_ref, users, total, residual, grad_in, held, ratings,
-    load_sem, rate_sem, slot_sem, send_sem, recv_sem, out_sem, grad_send, grad_recv,
+    load_sem, rate_sem, slot_sem, send_sem, recv_sem, out_sem, grad_sem, grad_send, grad_recv,
 ):
     rows, rank = users.shape
     items = held[0].shape[0]
@@ -86,20 +86,23 @@
     map_slots = pltpu.make_async_copy(slot_rows, slot_ref, slot_sem)
     map_slots.start()
 
-    def residuals(s, c, rounded):
-        for top in range(0, rows, BLOCK):
+    def residuals(s, c, rounded, start, size):
+        step = min(size, BLOCK)
+        for offset in range(0, size, step):
+            top = pl.multiple_of(start + offset, step)
             predicted = lax.dot_general(
-                users[top : top + BLOCK, :], rounded, (((1,), (1,)), ((), ())),
+                users[pl.ds(top, step), :], rounded, (((1,), (1,)), ((), ())),
                 preferred_element_type=jnp.float32,
             )
-            for i in range(BLOCK // TILE):
+            for i in range(step // TILE):
                 for j in range(wide):
                     slot = slot_ref[s, (top // TILE + i) * col_tiles + c * wide + j]
                     live = (slot < slots).astype(jnp.float32)
                     rated = ratings[s][jnp.minimum(slot, slots - 1)].astype(jnp.float32)
                     guess = predicted[i * TILE : (i + 1) * TILE, j * TILE : (j + 1) * TILE]
                     residual[
-                        top + i * TILE : top + (i + 1) * TILE, j * TILE : (j + 1) * TILE
+                        pl.ds(pl.multiple_of(top + i * TILE, TILE), TILE),
+                        j * TILE : (j + 1) * TILE,
                     ] = ((guess - rated) * live).astype(jnp.bfloat16)
 
     def update(s, c, panel):
@@ -132,7 +135,7 @@
                 send(s - 1, c).wait_recv()
             panel = held[s][part(c), :]
             rounded = panel.astype(jnp.bfloat16)
-            residuals(s, c, rounded)
+            residuals(s, c, rounded, 0, rows)
             update(s, c, panel)
             if s < steps - 1:
                 if s == 0:
@@ -159,42 +162,55 @@
 
         lax.fori_loop(0, chunks if s < steps - 1 else chunks - 1, work, 0)
 
-    def exchange(d):
+    block = min(share, BLOCK)
+
+    def exchange(d, b):
         peer = lax.rem(g + d, groups)
+        top = pl.multiple_of(peer * share + b * block, block)
         return pltpu.make_async_remote_copy(
-            src_ref=total.at[pl.ds(pl.multiple_of(peer * share, share), share)],
-            dst_ref=grad_in.at[d - 1],
-            send_sem=grad_send.at[d - 1],
-            recv_sem=grad_recv.at[d - 1],
+            src_ref=total.at[pl.ds(top, block)],
+            dst_ref=grad_in.at[d - 1, pl.ds(b * block, block)],
+            send_sem=grad_send.at[d - 1, b],
+            recv_sem=grad_recv.at[d - 1, b],
             device_id={"item": peer},
             device_id_type=MESH,
+        )
+
+    def finish(b):
+        here = pl.ds(pl.multiple_of(g * share + b * block, block), block)
+        return here, pltpu.make_async_copy(
+            total.at[here], grad_out.at[pl.ds(b * block, block)], grad_sem.at[b]
         )
 
     final, last = steps - 1, chunks - 1
     send(final - 1, last).wait_recv()
     panel = held[final][part(last), :]
     rounded = panel.astype(jnp.bfloat16)
-    residuals(final, last, rounded)
-    for d in range(1, groups):
-        add_users(rounded, lax.rem(g + d, groups) * share, share)
-        exchange(d).start()
+    parts = [(d, b) for d in range(1, groups) for b in range(share // block)]
+    for d, b in parts:
+        top = lax.rem(g + d, groups) * share + b * block
+        residuals(final, last, rounded, top, block)
+        add_users(rounded, top, block)
+        exchange(d, b).start()
+    residuals(final, last, rounded, g * share, share)
     update(final, last, panel)
     write(last).start()
     add_users(rounded, g * share, share)
-    mine = pl.ds(pl.multiple_of(g * share, share), share)
-    for d in range(1, groups):
-        exchange(d).wait_recv()
-        total[mine, :] += grad_in[d - 1]
-    total[mine, :] = user_scale * total[mine, :]
-    finish = pltpu.make_async_copy(total.at[mine], grad_out, load_sem.at[chunks])
-    finish.start()
-    for d in range(1, groups):
-        exchange(d).wait_send()
+    for b in range(share // block):
+        here, done = finish(b)
+        for d in range(1, groups):
+            exchange(d, b).wait_recv()
+            total[here, :] += grad_in[d - 1, pl.ds(b * block, block), :]
+        total[here, :] = user_scale * total[here, :]
+        done.start()
+    for d, b in parts:
+        exchange(d, b).wait_send()
     for c in range(chunks - FLIGHT, chunks):
         send(final - 1, c).wait_send()
     for c in range(chunks):
         write(c).wait()
-    finish.wait()
+    for b in range(share // block):
+        finish(b)[1].wait()
 
 
 def place(held, gradient, panel_out, grad_out, panel_sem, grad_sem):
@@ -220,6 +236,7 @@
     chunks = items // CHUNK
     tiles = (rows // TILE) * (items // TILE)
     share = rows // groups
+    blocks = share // min(share, BLOCK)
 
     ids = tile_ids.reshape(steps, 1, slots)
     count = tile_count.reshape(steps)
@@ -250,8 +267,9 @@
             pltpu.SemaphoreType.DMA((steps - 1, chunks)),
             pltpu.SemaphoreType.DMA((steps - 1, chunks)),
             pltpu.SemaphoreType.DMA((chunks,)),
-            pltpu.SemaphoreType.DMA((max(groups - 1, 1),)),
-            pltpu.SemaphoreType.DMA((max(groups - 1, 1),)),
+            pltpu.SemaphoreType.DMA((blocks,)),
+            pltpu.SemaphoreType.DMA((max(groups - 1, 1), blocks)),
+            pltpu.SemaphoreType.DMA((max(groups - 1, 1), blocks)),
         ],
         compiler_params=pltpu.CompilerParams(
             collective_id=0, has_side_effects=True, vmem_limit_bytes=56 * 2**20
@@ -270,8 +288,9 @@
         in_specs=[anywhere] * 2,
         out_specs=(anywhere, anywhere),
         scratch_shapes=[pltpu.SemaphoreType.DMA((PIECES,)), pltpu.SemaphoreType.DMA((PIECES,))],
+        compiler_params=pltpu.CompilerParams(vmem_limit_bytes=4 * 2**20),
         name="place",
-    )(held, gradient)
+    )(*(pltpu.with_memory_space_constraint(x, pltpu.VMEM) for x in (held, gradient)))
 
 
 def solution(mesh):

time: 109 us -> 59.8 us (0.55)
  Pallas kernels: 107 us -> 59 us
  local copies, waits for them, and re-layouts: 1.76 us -> 0 us
    pallas_call x1, Pallas kernels: 48.8 us -> 1.2 us  [shards(): pl.pallas_call(place, out_shape=(jax.ShapeDtypeStruct(held.shape, held.dt...]
    unnamed x4 -> x0, local copies, waits for them, and re-layouts: 1.76 us -> none
where the time goes in v1:
time: 59.8 us; the launch traced here: 59.7 us
  Pallas kernels  59 us (99%)
  between operations  0.64 us (1%)
    pallas_call x1, Pallas kernels, shards(): pl.pallas_call(functools.partial(kernel, steps, cycle, groups), out_shape...  57.8 us
    pallas_call x1, Pallas kernels, shards(): pl.pallas_call(place, out_shape=(jax.ShapeDtypeStruct(held.shape, held.dt...  1.2 us

profile of v1, /device:TPU:0, one launch (start us, length us, event | category | flops | bytes accessed | tf_op | source)
XLA Modules:
  0.0 59.7 jit_solution(3139984338214696491)
XLA Ops:
  0.6 57.8 %sub_epoch.1 = (f32[1024,256]{1,0:T(8,128)S(1)}, f32[512,256]{1,0:T(8,128)S(1)}) custom-call(s32[3,1,24]{2,1,0:T(1,128)} %bitcast.2, s32[3]{0:T(128)} %bitcast.3, bf16[1024,256]{1,0:T(8,128)(2,1)} %users_hbm.1, f32[1024,256]{1,0:T(8,128)} %panel_hbm.1, bf16[3,24,128,128]{3,2,1,0:T(8,128)(2,1)} %ratings_hbm.1), custom_call_target="tpu_custom_call" | custom-call | tf_op jit(solution)/shard_map/sub_epoch/pallas_call | solution.py:247
  58.5 1.2 %place.1 = (f32[1024,256]{1,0:T(8,128)}, f32[512,256]{1,0:T(8,128)}) custom-call(f32[1024,256]{1,0:T(8,128)S(1)} %get-tuple-element.4.held, f32[512,256]{1,0:T(8,128)S(1)} %get-tuple-element.5.gradient), custom_call_target="tpu_custom_call" | custom-call | tf_op jit(solution)/shard_map/place/pallas_call | solution.py:282

commit v2 on v1

--- a/solution.py
+++ b/solution.py
@@ -22,8 +22,9 @@
 def kernel(
     steps, cycle, groups,
     ids_ref, count_ref, users_hbm, panel_hbm, ratings_hbm, panel_out, grad_out,
-    slot_rows, slot_ref, users, total, residual, grad_in, held, ratings,
+    slot_rows, slot_ref, detour, users, total, residual, grad_in, held, ratings,
     load_sem, rate_sem, slot_sem, send_sem, recv_sem, out_sem, grad_sem, grad_send, grad_recv,
+    detour_send, detour_recv,
 ):
     rows, rank = users.shape
     items = held[0].shape[0]
@@ -43,6 +44,14 @@
         pl.semaphore_signal(
             barrier, inc=1, device_id={"item": lax.rem(g + d, groups)}, device_id_type=MESH
         )
+
+    first, helper, end = 0, 1, cycle - 1
+    helped = cycle > 3
+    if helped:
+        for source, target in ((first, helper), (helper, end)):
+            @pl.when(u == source)
+            def _(target=target):
+                pl.semaphore_signal(barrier, inc=1, device_id={"user": target}, device_id_type=MESH)
 
     def part(c):
         return pl.ds(pl.multiple_of(c * CHUNK, CHUNK), CHUNK)
@@ -70,6 +79,26 @@
             send_sem=send_sem.at[s, c],
             recv_sem=recv_sem.at[s, c],
             device_id={"user": right},
+            device_id_type=MESH,
+        )
+
+    def aside():
+        return pltpu.make_async_remote_copy(
+            src_ref=held[0].at[part(chunks - 1)],
+            dst_ref=detour,
+            send_sem=send_sem.at[0, chunks - 1],
+            recv_sem=detour_recv,
+            device_id={"user": helper},
+            device_id_type=MESH,
+        )
+
+    def onward():
+        return pltpu.make_async_remote_copy(
+            src_ref=detour,
+            dst_ref=held[1].at[part(chunks - 1)],
+            send_sem=detour_send,
+            recv_sem=recv_sem.at[0, chunks - 1],
+            device_id={"user": first},
             device_id_type=MESH,
         )
 
@@ -132,6 +161,11 @@
                     panel_hbm.at[part(c)], held[0].at[part(c)], load_sem.at[c]
                 ).wait()
             else:
+                if s == 1 and helped:
+                    @pl.when((u == helper) & (c == chunks // 2 + 1))
+                    def _():
+                        aside().wait_recv()
+                        onward().start()
                 send(s - 1, c).wait_recv()
             panel = held[s][part(c), :]
             rounded = panel.astype(jnp.bfloat16)
@@ -141,7 +175,18 @@
                 if s == 0:
                     @pl.when(c == 0)
                     def _():
-                        pl.semaphore_wait(barrier, groups)
+                        if helped:
+                            aiding = (u == helper) | (u == end)
+
+                            @pl.when(aiding)
+                            def _():
+                                pl.semaphore_wait(barrier, groups + 1)
+
+                            @pl.when(jnp.logical_not(aiding))
+                            def _():
+                                pl.semaphore_wait(barrier, groups)
+                        else:
+                            pl.semaphore_wait(barrier, groups)
 
                     @pl.when(c >= FLIGHT)
                     def _():
@@ -154,7 +199,18 @@
                     @pl.when(c < FLIGHT)
                     def _():
                         send(s - 1, chunks + c - FLIGHT).wait_send()
-                send(s, c).start()
+                if s == 0 and helped:
+                    parted = (u == end) & (c == chunks - 1)
+
+                    @pl.when(parted)
+                    def _():
+                        aside().start()
+
+                    @pl.when(jnp.logical_not(parted))
+                    def _():
+                        send(s, c).start()
+                else:
+                    send(s, c).start()
             else:
                 write(c).start()
             add_users(rounded, 0, rows)
@@ -207,6 +263,10 @@
         exchange(d, b).wait_send()
     for c in range(chunks - FLIGHT, chunks):
         send(final - 1, c).wait_send()
+    if helped:
+        @pl.when(u == helper)
+        def _():
+            onward().wait_send()
     for c in range(chunks):
         write(c).wait()
     for b in range(share // block):
@@ -255,6 +315,7 @@
         scratch_shapes=[
             pltpu.VMEM((steps, tiles), jnp.int32),
             pltpu.SMEM((steps, tiles), jnp.int32),
+            pltpu.VMEM((CHUNK, rank), jnp.float32),
             pltpu.VMEM((rows, rank), jnp.bfloat16),
             pltpu.VMEM((rows, rank), jnp.float32),
             pltpu.VMEM((rows, CHUNK), jnp.bfloat16),
@@ -270,6 +331,8 @@
             pltpu.SemaphoreType.DMA((blocks,)),
             pltpu.SemaphoreType.DMA((max(groups - 1, 1), blocks)),
             pltpu.SemaphoreType.DMA((max(groups - 1, 1), blocks)),
+            pltpu.SemaphoreType.DMA,
+            pltpu.SemaphoreType.DMA,
         ],
         compiler_params=pltpu.CompilerParams(
             collective_id=0, has_side_effects=True, vmem_limit_bytes=56 * 2**20

time: 59.8 us -> 59.9 us (level)
  no operation moved by 1% of the time
where the time goes in v2:
time: 59.9 us; the launch traced here: 59.7 us
  Pallas kernels  59.1 us (99%)
  between operations  0.64 us (1%)
    pallas_call x1, Pallas kernels, shards(): pl.pallas_call(functools.partial(kernel, steps, cycle, groups), out_shape...  57.9 us
    pallas_call x1, Pallas kernels, shards(): pl.pallas_call(place, out_shape=(jax.ShapeDtypeStruct(held.shape, held.dt...  1.2 us

profile of v2, /device:TPU:0, one launch (start us, length us, event | category | flops | bytes accessed | tf_op | source)
XLA Modules:
  0.0 59.7 jit_solution(8931223046915866750)
XLA Ops:
  0.6 57.9 %sub_epoch.1 = (f32[1024,256]{1,0:T(8,128)S(1)}, f32[512,256]{1,0:T(8,128)S(1)}) custom-call(s32[3,1,24]{2,1,0:T(1,128)} %bitcast.2, s32[3]{0:T(128)} %bitcast.3, bf16[1024,256]{1,0:T(8,128)(2,1)} %users_hbm.1, f32[1024,256]{1,0:T(8,128)} %panel_hbm.1, bf16[3,24,128,128]{3,2,1,0:T(8,128)(2,1)} %ratings_hbm.1), custom_call_target="tpu_custom_call" | custom-call | tf_op jit(solution)/shard_map/sub_epoch/pallas_call | solution.py:307
  58.5 1.2 %place.1 = (f32[1024,256]{1,0:T(8,128)}, f32[512,256]{1,0:T(8,128)}) custom-call(f32[1024,256]{1,0:T(8,128)S(1)} %get-tuple-element.4.held, f32[512,256]{1,0:T(8,128)S(1)} %get-tuple-element.5.gradient), custom_call_target="tpu_custom_call" | custom-call | tf_op jit(solution)/shard_map/place/pallas_call | solution.py:345

commit v3 on v1

--- a/solution.py
+++ b/solution.py
@@ -8,7 +8,7 @@
 from jax.sharding import PartitionSpec as P
 
 TILE = 128
-CHUNK = 128
+CHUNK = 256
 BLOCK = 256
 FLIGHT = 4
 PIECES = 4

time: 59.8 us -> 59.7 us (level)
  no operation moved by 1% of the time
where the time goes in v3:
time: 59.7 us; the launch traced here: 59.5 us
  Pallas kernels  58.8 us (98%)
  between operations  0.64 us (1%)
    pallas_call x1, Pallas kernels, shards(): pl.pallas_call(functools.partial(kernel, steps, cycle, groups), out_shape...  57.6 us
    pallas_call x1, Pallas kernels, shards(): pl.pallas_call(place, out_shape=(jax.ShapeDtypeStruct(held.shape, held.dt...  1.2 us

profile of v3, /device:TPU:0, one launch (start us, length us, event | category | flops | bytes accessed | tf_op | source)
XLA Modules:
  0.0 59.5 jit_solution(10032073181968556127)
XLA Ops:
  0.6 57.6 %sub_epoch.1 = (f32[1024,256]{1,0:T(8,128)S(1)}, f32[512,256]{1,0:T(8,128)S(1)}) custom-call(s32[3,1,24]{2,1,0:T(1,128)} %bitcast.2, s32[3]{0:T(128)} %bitcast.3, bf16[1024,256]{1,0:T(8,128)(2,1)} %users_hbm.1, f32[1024,256]{1,0:T(8,128)} %panel_hbm.1, bf16[3,24,128,128]{3,2,1,0:T(8,128)(2,1)} %ratings_hbm.1), custom_call_target="tpu_custom_call" | custom-call | tf_op jit(solution)/shard_map/sub_epoch/pallas_call | solution.py:247
  58.3 1.2 %place.1 = (f32[1024,256]{1,0:T(8,128)}, f32[512,256]{1,0:T(8,128)}) custom-call(f32[1024,256]{1,0:T(8,128)S(1)} %get-tuple-element.4.held, f32[512,256]{1,0:T(8,128)S(1)} %get-tuple-element.5.gradient), custom_call_target="tpu_custom_call" | custom-call | tf_op jit(solution)/shard_map/place/pallas_call | solution.py:282

commit v4 on v3

--- a/solution.py
+++ b/solution.py
@@ -10,7 +10,7 @@
 TILE = 128
 CHUNK = 256
 BLOCK = 256
-FLIGHT = 4
+FLIGHT = 2
 PIECES = 4
 MESH = pl.DeviceIdType.MESH
 

time: 59.7 us -> 59.7 us (level)
  no operation moved by 1% of the time
where the time goes in v4:
time: 59.7 us; the launch traced here: 59.5 us
  Pallas kernels  58.8 us (98%)
  between operations  0.64 us (1%)
    pallas_call x1, Pallas kernels, shards(): pl.pallas_call(functools.partial(kernel, steps, cycle, groups), out_shape...  57.6 us
    pallas_call x1, Pallas kernels, shards(): pl.pallas_call(place, out_shape=(jax.ShapeDtypeStruct(held.shape, held.dt...  1.2 us

profile of v4, /device:TPU:0, one launch (start us, length us, event | category | flops | bytes accessed | tf_op | source)
XLA Modules:
  0.0 59.5 jit_solution(16489290981565691830)
XLA Ops:
  0.6 57.6 %sub_epoch.1 = (f32[1024,256]{1,0:T(8,128)S(1)}, f32[512,256]{1,0:T(8,128)S(1)}) custom-call(s32[3,1,24]{2,1,0:T(1,128)} %bitcast.2, s32[3]{0:T(128)} %bitcast.3, bf16[1024,256]{1,0:T(8,128)(2,1)} %users_hbm.1, f32[1024,256]{1,0:T(8,128)} %panel_hbm.1, bf16[3,24,128,128]{3,2,1,0:T(8,128)(2,1)} %ratings_hbm.1), custom_call_target="tpu_custom_call" | custom-call | tf_op jit(solution)/shard_map/sub_epoch/pallas_call | solution.py:247
  58.3 1.2 %place.1 = (f32[1024,256]{1,0:T(8,128)}, f32[512,256]{1,0:T(8,128)}) custom-call(f32[1024,256]{1,0:T(8,128)S(1)} %get-tuple-element.4.held, f32[512,256]{1,0:T(8,128)S(1)} %get-tuple-element.5.gradient), custom_call_target="tpu_custom_call" | custom-call | tf_op jit(solution)/shard_map/place/pallas_call | solution.py:282

commit v5 on v4

--- a/solution.py
+++ b/solution.py
@@ -58,10 +58,6 @@
     load_panel[0].start()
     load_users.start()
     load_rates[0].start()
-    for c in range(1, chunks):
-        load_panel[c].start()
-    for s in range(1, steps):
-        load_rates[s].start()
 
     def send(s, c):
         return pltpu.make_async_remote_copy(
@@ -125,6 +121,11 @@
     load_users.wait()
     for s in range(steps):
         load_rates[s].wait()
+        if s == 0:
+            for c in range(1, chunks):
+                load_panel[c].start()
+        if s < steps - 1:
+            load_rates[s + 1].start()
 
         def work(c, carry, s=s):
             if s == 0:

time: 59.7 us -> 59.7 us (level)
  no operation moved by 1% of the time
where the time goes in v5:
time: 59.7 us; the launch traced here: 59.5 us
  Pallas kernels  58.9 us (99%)
  between operations  0.64 us (1%)
    pallas_call x1, Pallas kernels, shards(): pl.pallas_call(functools.partial(kernel, steps, cycle, groups), out_shape...  57.7 us
    pallas_call x1, Pallas kernels, shards(): pl.pallas_call(place, out_shape=(jax.ShapeDtypeStruct(held.shape, held.dt...  1.2 us

profile of v5, /device:TPU:0, one launch (start us, length us, event | category | flops | bytes accessed | tf_op | source)
XLA Modules:
  0.0 59.5 jit_solution(5652336355109121814)
XLA Ops:
  0.6 57.7 %sub_epoch.1 = (f32[1024,256]{1,0:T(8,128)S(1)}, f32[512,256]{1,0:T(8,128)S(1)}) custom-call(s32[3,1,24]{2,1,0:T(1,128)} %bitcast.2, s32[3]{0:T(128)} %bitcast.3, bf16[1024,256]{1,0:T(8,128)(2,1)} %users_hbm.1, f32[1024,256]{1,0:T(8,128)} %panel_hbm.1, bf16[3,24,128,128]{3,2,1,0:T(8,128)(2,1)} %ratings_hbm.1), custom_call_target="tpu_custom_call" | custom-call | tf_op jit(solution)/shard_map/sub_epoch/pallas_call | solution.py:248
  58.3 1.2 %place.1 = (f32[1024,256]{1,0:T(8,128)}, f32[512,256]{1,0:T(8,128)}) custom-call(f32[1024,256]{1,0:T(8,128)S(1)} %get-tuple-element.4.held, f32[512,256]{1,0:T(8,128)S(1)} %get-tuple-element.5.gradient), custom_call_target="tpu_custom_call" | custom-call | tf_op jit(solution)/shard_map/place/pallas_call | solution.py:283
